TPU v7x, 32 devices: a whole 2x2x4 slice. The times are simulated.
32 devices in a mesh: reach: 8 (over z, y), ens: 4 (over x, core).
Axes of the slice: x: 2, y: 2, z: 4, core: 2. Of those that a mesh axis runs over, the one named last changes fastest.
Arguments:
- adjoint: float32 [16, 3, 64, 1024], P('ens', None, None, 'reach'), may hold values from -6 to 6
- momentum: bfloat16 [16, 2, 64, 1024], P('ens', None, None, 'reach'), may hold values from -6 to 6
- friction: float32 [64, 1024], P(None, 'reach'), may hold values from 10 to 100
- roughness: float32 [128], replicated, may hold values from 0.02 to 0.1
- geometry: float32 [2, 1024], P(None, 'reach'), may hold values from 0.5 to 2
- face_scale: float32 [4, 1024], P(None, 'reach'), may hold values from 0.5 to 2
- vol_blocks: float32 [2, 64, 64], replicated, may hold values from -0.75 to 0.75
- face_blocks: float32 [4, 64, 64], replicated, may hold values from -0.75 to 0.75
- flux_mix: float32 [2, 3, 3], replicated, may hold values from -3.5 to 3.5
- neighbours: int32 [4, 1024], P(None, 'reach'), may hold values from -1 to 1023, as said below
- patch_map: int32 [1024], P('reach'), may hold values from 0 to 127
- patch_owner: int32 [128], replicated, may hold values from 0 to 7, as said below
- wet: int32 [1024], P('reach'), may hold values 0 or 1
Outputs:
- finals: float32 [16, 3, 64, 1024], P('ens', None, None, 'reach')
- owned: float32 [256], P('reach')
Inputs may be any that keep to these rules, and one draw needn't show every extreme that they name: `neighbours`: each entry is -1 or an element index at most 32 positions from the element's own index. `patch_owner`: each owner holds at most 32 patches, and some owner holds exactly 32.
All inputs are finite; a program needn't handle non-finite values. No bound on the sum of `wet` on one device may be relied on, other than what follows from the above.
Results may differ from a plain program's by a relative error of at most 0.0003.
Values sent between devices are 32-bit elements; how exact they have to be, the bound alone decides.
A program may use at most 64 MiB of HBM per device.

v0:
```python
import functools

import jax
import jax.numpy as jnp
from jax import lax
from jax.experimental import pallas as pl
from jax.experimental.pallas import tpu as pltpu
from jax.sharding import PartitionSpec as P

RIVW = 32
STEPS = 2
OWN_MAX = 32
TIME_STEP = 0.05
F32 = jnp.float32
BF16 = jnp.bfloat16
FINEST = lax.Precision.HIGHEST
NAMED = pl.DeviceIdType.MESH


def split_two(x):
    hi = x.astype(BF16)
    return hi, (x - hi.astype(F32)).astype(BF16)


def radices(count):
    out = []
    while count > 1:
        size = next(r for r in (8, 7, 6, 5, 4, 3, 2, count) if count % r == 0)
        out.append(size)
        count //= size
    return out


def kernel(
    n_reach, n_ens, members_all,
    adj_ref, mom_ref, fric_ref, rough_ref, geo_ref, face_ref, vol_ref, fb_ref, mix_ref,
    nb_ref, pm_ref, po_ref, wet_ref,
    out_ref, own_ref,
    lam, hal, acc, sel, w_all, dscale, damp, onehot, snd, rcv, psnd, prcv,
    snd_sem, rcv_sem, psnd_sem, prcv_sem,
):
    members, comps, nodes, elems = adj_ref.shape
    npatch = rough_ref.shape[1]
    me = lax.axis_index("reach")
    my_ens = lax.axis_index("ens")
    groups = elems // RIVW
    prows = nodes // groups
    digits = radices(n_reach)

    phases = [("ens", n_ens, my_ens, 1)]
    stride = 1
    for size in digits:
        phases.append(("reach", size, lax.rem(lax.div(me, stride), size), stride))
        stride *= size

    def partner(phase, k):
        axis, size, mine, step = phases[phase]
        other = lax.rem(mine + k, size)
        base = my_ens if axis == "ens" else me
        return {axis: base + (other - mine) * step}

    barrier = pltpu.get_barrier_semaphore()
    expected = 0
    for phase in range(len(phases)):
        for k in range(1, phases[phase][1]):
            pl.semaphore_signal(barrier, inc=1, device_id=partner(phase, k), device_id_type=NAMED)
            expected += 1
    far = len(digits) > 1
    if far:
        @pl.when(me > 0)
        def _():
            pl.semaphore_signal(barrier, inc=1, device_id={"reach": me - 1}, device_id_type=NAMED)

        @pl.when(me < n_reach - 1)
        def _():
            pl.semaphore_signal(barrier, inc=1, device_id={"reach": me + 1}, device_id_type=NAMED)

    lane = lax.broadcasted_iota(jnp.int32, (prows, elems), 1)

    def halo_copy(stage, side, m):
        to = me + 1 if side == 0 else me - 1
        return pltpu.make_async_remote_copy(
            src_ref=snd.at[stage, side, m],
            dst_ref=rcv.at[stage, side, m],
            send_sem=snd_sem.at[stage, side, m],
            recv_sem=rcv_sem.at[stage, side, m],
            device_id={"reach": to},
            device_id_type=NAMED,
        )

    def pack(stage, m, c, x):
        for side in range(2):
            packed = None
            for g in range(groups):
                rows = x[g * prows:(g + 1) * prows]
                shift = (RIVW * g - (elems - RIVW if side == 0 else 0)) % elems
                moved = pltpu.roll(rows, shift, 1) if shift else rows
                packed = moved if packed is None else jnp.where(lane >= g * RIVW, moved, packed)
            snd[stage, side, m, c * prows:(c + 1) * prows, :] = packed

    def send(stage, m):
        @pl.when(me < n_reach - 1)
        def _():
            halo_copy(stage, 0, m).start()

        @pl.when(me > 0)
        def _():
            halo_copy(stage, 1, m).start()

    def receive(stage, m):
        @pl.when(me > 0)
        def _():
            halo_copy(stage, 0, m).wait_recv()

        @pl.when(me < n_reach - 1)
        def _():
            halo_copy(stage, 1, m).wait_recv()

    def work(m, c, x):
        if c == 0:
            return None
        return mom_ref[m, c - 1].astype(F32) * x

    for m in range(members):
        for c in range(comps):
            pack(0, m, c, adj_ref[m, c])

    pl.semaphore_wait(barrier, expected)
    if far:
        @pl.when(me > 0)
        def _():
            pl.semaphore_wait(barrier, 1)

        @pl.when(me < n_reach - 1)
        def _():
            pl.semaphore_wait(barrier, 1)
    for m in range(members):
        send(0, m)

    @pl.when(me == 0)
    def _():
        rcv[:, 0] = jnp.zeros(rcv.shape[:1] + rcv.shape[2:], F32)

    @pl.when(me == n_reach - 1)
    def _():
        rcv[:, 1] = jnp.zeros(rcv.shape[:1] + rcv.shape[2:], F32)

    wet = wet_ref[...].astype(F32)
    wet_dt = TIME_STEP * wet
    patch_row = lax.broadcasted_iota(jnp.int32, (npatch, elems), 0)
    onehot[...] = jnp.where(patch_row == pm_ref[...], 1.0, 0.0).astype(F32)
    rough8 = jnp.broadcast_to(rough_ref[...], (8, npatch))
    rough = jnp.dot(rough8, onehot[...], precision=FINEST, preferred_element_type=F32)[0:1]
    damp[...] = (wet_dt * rough * rough) * fric_ref[...]
    for d in range(2):
        dscale[d:d + 1, :] = wet_dt * geo_ref[d:d + 1, :]
    for f in range(4):
        dscale[2 + f:3 + f, :] = wet_dt * face_ref[f:f + 1, :]

    src_row = lax.broadcasted_iota(jnp.int32, (2 * elems, elems), 0)
    src_col = lax.broadcasted_iota(jnp.int32, (2 * elems, elems), 1)
    itself = jnp.where(src_row == src_col, 1.0, 0.0)
    for f in range(4):
        nb = nb_ref[f:f + 1, :]
        local = nb - me * elems
        row = jnp.where(local < 0, local + elems + RIVW, jnp.where(local < elems, local, local + elems - RIVW))
        row = jnp.where(nb >= 0, row, -1)
        hit = jnp.where(src_row == row, 1.0, 0.0)
        own = jnp.where(nb >= 0, 1.0, 0.0) * itself
        sel[:, f * elems:(f + 1) * elems] = (hit - own).astype(BF16)

    for b in range(6):
        block = vol_ref[b] if b < 2 else fb_ref[b - 2]
        hi, lo = split_two(block)
        w_all[0:nodes, b * nodes:(b + 1) * nodes] = hi
        w_all[nodes:2 * nodes, b * nodes:(b + 1) * nodes] = lo

    first = None
    for m in range(members):
        for c in range(1, comps):
            term = work(m, c, adj_ref[m, c])
            first = term if first is None else first + term
    acc[...] = first

    mix = [[[mix_ref[d, a, c] for c in range(comps)] for a in range(comps)] for d in range(2)]

    def body(stage, src, m):
        receive(stage, m)
        state = [src[m, c] for c in range(comps)]
        ghost = []
        for c in range(comps):
            west = rcv[stage, 0, m, c * prows:(c + 1) * prows, :]
            east = rcv[stage, 1, m, c * prows:(c + 1) * prows, :]
            for g in range(groups):
                a, b = (-RIVW * g) % elems, (elems - RIVW - RIVW * g) % elems
                wr = pltpu.roll(west, a, 1) if a else west
                er = pltpu.roll(east, b, 1) if b else east
                ghost.append(jnp.where(lane < elems // 2, wr, er))
        full = jnp.concatenate(
            [jnp.concatenate(state, axis=0), jnp.concatenate(ghost, axis=0)], axis=1
        )
        hi, lo = split_two(full)
        jump = jnp.dot(hi, sel[...], preferred_element_type=F32)
        jump = jump + jnp.dot(lo, sel[...], preferred_element_type=F32)
        cols_hi, cols_lo = [], []
        for c in range(comps):
            pieces = []
            for d in range(2):
                z = mix[d][0][c] * state[0] + mix[d][1][c] * state[1] + mix[d][2][c] * state[2]
                pieces.append(dscale[d:d + 1, :] * z)
            for f in range(4):
                pieces.append(
                    dscale[2 + f:3 + f, :]
                    * jump[c * nodes:(c + 1) * nodes, f * elems:(f + 1) * elems]
                )
            data = jnp.concatenate(pieces, axis=0)
            dh, dl = split_two(data)
            cols_hi.append(dh)
            cols_lo.append(dl)
        data_hi = jnp.concatenate(cols_hi, axis=1)
        data_lo = jnp.concatenate(cols_lo, axis=1)
        both = jnp.dot(w_all[...], data_hi, preferred_element_type=F32)
        total = both[:nodes] + both[nodes:]
        total = total + jnp.dot(w_all[0:nodes, :], data_lo, preferred_element_type=F32)
        moved = []
        for c in range(comps):
            inc = total[:, c * elems:(c + 1) * elems]
            if c > 0:
                inc = inc - damp[...] * state[c]
            moved.append(state[c] + inc)
        return moved

    last = 2 * STEPS - 1

    def stage_member(stage, m):
        step, half = divmod(stage, 2)
        base = adj_ref if step == 0 else lam
        if half == 0:
            new = body(stage, base, m)
            for c in range(comps):
                hal[m, c] = new[c]
        else:
            new = body(stage, hal, m)
            new = [0.5 * base[m, c] + 0.5 * new[c] for c in range(comps)]
            dst = out_ref if stage == last else lam
            for c in range(comps):
                dst[m, c] = new[c]
        if stage < last:
            for c in range(comps):
                pack(stage + 1, m, c, new[c])
            send(stage + 1, m)
            acc[...] += work(m, 1, new[1]) + work(m, 2, new[2])

    def run(stage, lo, hi):
        def step(m, carry):
            stage_member(stage, m)
            return carry

        lax.fori_loop(lo, hi, step, 0)

    def patch_copy(phase, k):
        mine = phases[phase][2]
        return pltpu.make_async_remote_copy(
            src_ref=psnd.at[phase],
            dst_ref=prcv.at[phase, mine],
            send_sem=psnd_sem.at[phase, k],
            recv_sem=prcv_sem.at[phase, k],
            device_id=partner(phase, k),
            device_id_type=NAMED,
        )

    def patch_send(phase, value):
        psnd[phase] = value
        prcv[phase, phases[phase][2]] = value
        for k in range(1, phases[phase][1]):
            patch_copy(phase, k).start()

    def patch_sum(phase):
        for k in range(1, phases[phase][1]):
            patch_copy(phase, k).wait_recv()
        total = prcv[phase, 0]
        for k in range(1, phases[phase][1]):
            total = total + prcv[phase, k]
        return total

    for stage in range(last):
        run(stage, 0, members)

    per_element = jnp.sum(fric_ref[...] * acc[...], axis=0, keepdims=True) * (-2.0 * wet * rough)
    sums = lax.dot_general(
        jnp.broadcast_to(per_element, (8, elems)), onehot[...], (((1,), (1,)), ((), ())),
        precision=FINEST, preferred_element_type=F32,
    )
    patch_send(0, sums)
    half_way = members // 2
    run(last, 0, half_way)
    for phase in range(1, len(phases)):
        patch_send(phase, patch_sum(phase - 1))
    run(last, half_way, members)
    sums = patch_sum(len(phases) - 1) * (1.0 / (members_all * nodes))

    slot_lanes = 128
    chunk = min(npatch, 128)
    tri = jnp.where(
        lax.broadcasted_iota(jnp.int32, (chunk, chunk), 0)
        < lax.broadcasted_iota(jnp.int32, (chunk, chunk), 1), 1.0, 0.0,
    )
    slot = lax.broadcasted_iota(jnp.int32, (slot_lanes, chunk), 0).astype(F32)
    before = jnp.zeros((1, 1), F32)
    result = jnp.zeros((8, slot_lanes), F32)
    for k in range(npatch // chunk):
        mine = jnp.where(po_ref[:, k * chunk:(k + 1) * chunk] == me, 1.0, 0.0)
        rank = jnp.dot(jnp.broadcast_to(mine, (8, chunk)), tri, preferred_element_type=F32)[0:1] + before
        table = jnp.where(slot == rank, 1.0, 0.0) * mine
        result = result + lax.dot_general(
            sums[:, k * chunk:(k + 1) * chunk], table, (((1,), (1,)), ((), ())),
            precision=FINEST, preferred_element_type=F32,
        )
        before = before + jnp.sum(mine, axis=1, keepdims=True)
    own_ref[...] = result[0:1, :OWN_MAX]

    for stage in range(2 * STEPS):
        for m in range(members):
            @pl.when(me < n_reach - 1)
            def _(stage=stage, m=m):
                halo_copy(stage, 0, m).wait_send()

            @pl.when(me > 0)
            def _(stage=stage, m=m):
                halo_copy(stage, 1, m).wait_send()
    for phase in range(len(phases)):
        for k in range(1, phases[phase][1]):
            patch_copy(phase, k).wait_send()


def shards(
    n_reach, n_ens,
    adjoint, momentum, friction, roughness, geometry, face_scale, vol_blocks, face_blocks,
    flux_mix, neighbours, patch_map, patch_owner, wet,
):
    members, comps, nodes, elems = adjoint.shape
    npatch = roughness.shape[0]
    stages = 2 * STEPS
    prow = comps * nodes * RIVW // elems
    sizes = [n_ens] + radices(n_reach)
    vmem = pl.BlockSpec(memory_space=pltpu.VMEM)
    specs = [vmem] * 13
    specs[8] = pl.BlockSpec(memory_space=pltpu.SMEM)
    finals, owned = pl.pallas_call(
        functools.partial(kernel, n_reach, n_ens, members * n_ens),
        out_shape=(
            jax.ShapeDtypeStruct(adjoint.shape, F32),
            jax.ShapeDtypeStruct((1, OWN_MAX), F32),
        ),
        in_specs=specs,
        out_specs=(vmem, vmem),
        scratch_shapes=[
            pltpu.VMEM(adjoint.shape, F32),
            pltpu.VMEM(adjoint.shape, F32),
            pltpu.VMEM((nodes, elems), F32),
            pltpu.VMEM((2 * elems, 4 * elems), BF16),
            pltpu.VMEM((2 * nodes, 6 * nodes), BF16),
            pltpu.VMEM((8, elems), F32),
            pltpu.VMEM((nodes, elems), F32),
            pltpu.VMEM((npatch, elems), F32),
            pltpu.VMEM((stages, 2, members, prow, elems), F32),
            pltpu.VMEM((stages, 2, members, prow, elems), F32),
            pltpu.VMEM((len(sizes), 8, npatch), F32),
            pltpu.VMEM((len(sizes), max(sizes), 8, npatch), F32),
            pltpu.SemaphoreType.DMA((stages, 2, members)),
            pltpu.SemaphoreType.DMA((stages, 2, members)),
            pltpu.SemaphoreType.DMA((len(sizes), max(sizes))),
            pltpu.SemaphoreType.DMA((len(sizes), max(sizes))),
        ],
        compiler_params=pltpu.CompilerParams(
            collective_id=0, has_side_effects=True, vmem_limit_bytes=40 * 1024 * 1024
        ),
    )(
        adjoint, momentum, friction, roughness.reshape(1, npatch), geometry, face_scale,
        vol_blocks, face_blocks, flux_mix, neighbours, patch_map.reshape(1, elems),
        patch_owner.reshape(1, npatch), wet.reshape(1, elems),
    )
    return finals, owned.reshape(OWN_MAX)


def solution(mesh):
    return jax.shard_map(
        functools.partial(shards, mesh.shape["reach"], mesh.shape["ens"]),
        mesh=mesh,
        in_specs=(
            P("ens", None, None, "reach"),
            P("ens", None, None, "reach"),
            P(None, "reach"),
            P(),
            P(None, "reach"),
            P(None, "reach"),
            P(),
            P(),
            P(),
            P(None, "reach"),
            P("reach"),
            P(),
            P("reach"),
        ),
        out_specs=(P("ens", None, None, "reach"), P("reach")),
        check_vma=False,
    )
```

profile of v0, /device:TPU:0, one launch (start us, length us, event | category | flops | bytes accessed | tf_op | source)
XLA Modules:
  0.0 38.9 jit_solution(6286002242905102332)
XLA Ops:
  0.6 0.0 copy-start.12
  0.6 0.7 %copy-done.12 = f32[2,3,3]{2,0,1:T(2,128)S(1)} copy-done((f32[2,3,3]{2,0,1:T(2,128)S(1)}, f32[2,3,3]{2,0,1:T(2,128)}, u32[]{:S(2)}) %copy-start.12) | copy-done | bytes 96
  1.3 0.0 copy-start.5
  1.3 0.0 copy-start.6
  1.3 0.0 copy-start.7
  1.3 0.0 copy-start.8
  1.3 0.0 copy-start.9
  1.3 0.0 copy-start.10
  1.3 0.0 copy-start.11
  1.4 0.6 %copy-done.5 = f32[4,128]{1,0:T(4,128)S(1)} copy-done((f32[4,128]{1,0:T(4,128)S(1)}, f32[4,128]{1,0:T(4,128)}, u32[]{:S(2)}) %copy-start.5) | copy-done | bytes 2072
  2.0 0.0 copy-done.6
  2.0 0.0 copy-done.7
  2.0 0.0 copy-done.8
  2.0 0.0 copy-done.9
  2.0 0.0 copy-done.10
  2.1 0.0 copy-done.11
  2.1 0.0 copy-start
  2.1 1.0 %copy-done = f32[4,3,64,128]{3,2,1,0:T(8,128)S(1)} copy-done((f32[4,3,64,128]{3,2,1,0:T(8,128)S(1)}, f32[4,3,64,128]{3,2,1,0:T(8,128)}, u32[]{:S(2)}) %copy-start) | copy-done | bytes 393240
  3.1 0.0 copy-start.1
  3.1 0.9 %copy-done.1 = bf16[4,2,64,128]{3,2,1,0:T(8,128)(2,1)S(1)} copy-done((bf16[4,2,64,128]{3,2,1,0:T(8,128)(2,1)S(1)}, bf16[4,2,64,128]{3,2,1,0:T(8,128)(2,1)}, u32[]{:S(2)}) %copy-start.1) | copy-done | bytes 131096
  4.0 0.0 copy-start.2
  4.0 0.9 %copy-done.2 = f32[4,64,64]{2,1,0:T(8,128)S(1)} copy-done((f32[4,64,64]{2,1,0:T(8,128)S(1)}, f32[4,64,64]{2,1,0:T(8,128)}, u32[]{:S(2)}) %copy-start.2) | copy-done | bytes 65560
  4.9 0.0 copy-start.3
  4.9 0.8 %copy-done.3 = f32[2,64,64]{2,1,0:T(8,128)S(1)} copy-done((f32[2,64,64]{2,1,0:T(8,128)S(1)}, f32[2,64,64]{2,1,0:T(8,128)}, u32[]{:S(2)}) %copy-start.3) | copy-done | bytes 32792
  5.7 0.0 copy-start.4
  5.7 0.8 %copy-done.4 = f32[64,128]{1,0:T(8,128)S(1)} copy-done((f32[64,128]{1,0:T(8,128)S(1)}, f32[64,128]{1,0:T(8,128)}, u32[]{:S(2)}) %copy-start.4) | copy-done | bytes 32792
  6.5 31.2 %shard_map.140 = (f32[4,3,64,128]{3,2,1,0:T(8,128)S(1)}, f32[1,32]{1,0:T(1,128)S(1)}) custom-call(f32[4,3,64,128]{3,2,1,0:T(8,128)S(1)} %copy-done, bf16[4,2,64,128]{3,2,1,0:T(8,128)(2,1)S(1)} %copy-done.1, f32[64,128]{1,0:T(8,128)S(1)} %copy-done.4, f32[1,128]{1,0:T(1,128)S(1)} %bitcast.5, f32[2,128]{1,0:T(2,128)S(1)} %copy-done.7, f32[4,128]{1,0:T(4,128)S(1)} %copy-done.5, ...), custom_call_target="tpu_custom_call" | custom-call | tf_op jit(solution)/shard_map/pallas_call | solution.py:349
  37.7 0.7 %copy.18 = f32[4,3,64,128]{3,2,1,0:T(8,128)} copy(f32[4,3,64,128]{3,2,1,0:T(8,128)S(1)} %get-tuple-element.8) | data formatting | bytes 786432
  38.4 0.5 %copy.19 = f32[32]{0:T(128)} copy(f32[32]{0:T(128)S(1)} %bitcast.9) | data formatting | bytes 256
  (1 shorter events, 0.0 us)
Async XLA Ops:
  0.6 0.7 %copy-start.12 = (f32[2,3,3]{2,0,1:T(2,128)S(1)}, f32[2,3,3]{2,0,1:T(2,128)}, u32[]{:S(2)}) copy-start(f32[2,3,3]{2,0,1:T(2,128)} %param.21) | copy-start | bytes 220
  1.3 0.7 %copy-start.5 = (f32[4,128]{1,0:T(4,128)S(1)}, f32[4,128]{1,0:T(4,128)}, u32[]{:S(2)}) copy-start(f32[4,128]{1,0:T(4,128)} %face_ref.1) | copy-start | bytes 6148
  1.3 0.7 %copy-start.6 = (s32[4,128]{1,0:T(4,128)S(1)}, s32[4,128]{1,0:T(4,128)}, u32[]{:S(2)}) copy-start(s32[4,128]{1,0:T(4,128)} %nb_ref.1) | copy-start | bytes 6148
  1.3 0.7 %copy-start.7 = (f32[2,128]{1,0:T(2,128)S(1)}, f32[2,128]{1,0:T(2,128)}, u32[]{:S(2)}) copy-start(f32[2,128]{1,0:T(2,128)} %geo_ref.1) | copy-start | bytes 3076
  1.3 0.7 %copy-start.8 = (f32[128]{0:T(128)S(1)}, f32[128]{0:T(128)}, u32[]{:S(2)}) copy-start(f32[128]{0:T(128)} %param.16) | copy-start | bytes 1540
  1.3 0.7 %copy-start.9 = (s32[128]{0:T(128)S(1)}, s32[128]{0:T(128)}, u32[]{:S(2)}) copy-start(s32[128]{0:T(128)} %param.23) | copy-start | bytes 1540
  1.3 0.7 %copy-start.10 = (s32[128]{0:T(128)S(1)}, s32[128]{0:T(128)}, u32[]{:S(2)}) copy-start(s32[128]{0:T(128)} %param.24) | copy-start | bytes 1540
  1.3 0.7 %copy-start.11 = (s32[128]{0:T(128)S(1)}, s32[128]{0:T(128)}, u32[]{:S(2)}) copy-start(s32[128]{0:T(128)} %param.25) | copy-start | bytes 1540
  2.1 1.0 %copy-start = (f32[4,3,64,128]{3,2,1,0:T(8,128)S(1)}, f32[4,3,64,128]{3,2,1,0:T(8,128)}, u32[]{:S(2)}) copy-start(f32[4,3,64,128]{3,2,1,0:T(8,128)} %adj_ref.1) | copy-start | bytes 1179652
  3.1 0.9 %copy-start.1 = (bf16[4,2,64,128]{3,2,1,0:T(8,128)(2,1)S(1)}, bf16[4,2,64,128]{3,2,1,0:T(8,128)(2,1)}, u32[]{:S(2)}) copy-start(bf16[4,2,64,128]{3,2,1,0:T(8,128)(2,1)} %mom_ref.1) | copy-start | bytes 393220
  4.0 0.9 %copy-start.2 = (f32[4,64,64]{2,1,0:T(8,128)S(1)}, f32[4,64,64]{2,1,0:T(8,128)}, u32[]{:S(2)}) copy-start(f32[4,64,64]{2,1,0:T(8,128)} %fb_ref.1) | copy-start | bytes 196612
  4.9 0.8 %copy-start.3 = (f32[2,64,64]{2,1,0:T(8,128)S(1)}, f32[2,64,64]{2,1,0:T(8,128)}, u32[]{:S(2)}) copy-start(f32[2,64,64]{2,1,0:T(8,128)} %vol_ref.1) | copy-start | bytes 98308
  5.7 0.8 %copy-start.4 = (f32[64,128]{1,0:T(8,128)S(1)}, f32[64,128]{1,0:T(8,128)}, u32[]{:S(2)}) copy-start(f32[64,128]{1,0:T(8,128)} %fric_ref.1) | copy-start | bytes 98308
where the time goes:
time: 39.3 us; the launch traced here: 38.9 us
  Pallas kernels  31.2 us (79%)
  local copies, waits for them, and re-layouts  7.05 us (18%)
  between operations  0.7 us (2%)
    pallas_call x1, Pallas kernels, shards(): pl.pallas_call(functools.partial(kernel, n_reach, n_ens, members * n_ens)...  31.2 us
    unnamed x29, local copies, waits for them, and re-layouts  7.05 us

commit v1 on v0

--- a/solution.py
+++ b/solution.py
@@ -13,6 +13,7 @@
 TIME_STEP = 0.05
 F32 = jnp.float32
 BF16 = jnp.bfloat16
+GROUP = 1
 FINEST = lax.Precision.HIGHEST
 NAMED = pl.DeviceIdType.MESH
 
@@ -33,13 +34,15 @@
 
 def kernel(
     n_reach, n_ens, members_all,
-    adj_ref, mom_ref, fric_ref, rough_ref, geo_ref, face_ref, vol_ref, fb_ref, mix_ref,
-    nb_ref, pm_ref, po_ref, wet_ref,
+    adj_hbm, mom_hbm, fric_hbm, rough_hbm, geo_hbm, face_hbm, vol_hbm, fb_hbm, mix_hbm,
+    nb_hbm, pm_hbm, po_hbm, wet_hbm,
     out_ref, own_ref,
+    mom_ref, fric_ref, rough_ref, geo_ref, face_ref, vol_ref, fb_ref, mix_ref,
+    nb_ref, pm_ref, po_ref, wet_ref, in_sem,
     lam, hal, acc, sel, w_all, dscale, damp, onehot, snd, rcv, psnd, prcv,
-    snd_sem, rcv_sem, psnd_sem, prcv_sem,
+    snd_sem, rcv_sem, psnd_sem, prcv_sem, table, out_sem,
 ):
-    members, comps, nodes, elems = adj_ref.shape
+    members, comps, nodes, elems = lam.shape
     npatch = rough_ref.shape[1]
     me = lax.axis_index("reach")
     my_ens = lax.axis_index("ens")
@@ -74,6 +77,21 @@
         @pl.when(me < n_reach - 1)
         def _():
             pl.semaphore_signal(barrier, inc=1, device_id={"reach": me + 1}, device_id_type=NAMED)
+
+    state_in = [
+        pltpu.make_async_copy(adj_hbm.at[m], lam.at[m], in_sem.at[m]) for m in range(members)
+    ]
+    tables_in = [
+        pltpu.make_async_copy(src, dst, in_sem.at[members + i])
+        for i, (src, dst) in enumerate([
+            (nb_hbm, nb_ref), (pm_hbm, pm_ref), (rough_hbm, rough_ref), (wet_hbm, wet_ref),
+            (fric_hbm, fric_ref), (geo_hbm, geo_ref), (face_hbm, face_ref),
+            (vol_hbm, vol_ref), (fb_hbm, fb_ref), (mom_hbm, mom_ref), (mix_hbm, mix_ref),
+            (po_hbm, po_ref),
+        ])
+    ]
+    for copy in state_in + tables_in:
+        copy.start()
 
     lane = lax.broadcasted_iota(jnp.int32, (prows, elems), 1)
 
@@ -122,19 +140,19 @@
         return mom_ref[m, c - 1].astype(F32) * x
 
     for m in range(members):
+        state_in[m].wait()
         for c in range(comps):
-            pack(0, m, c, adj_ref[m, c])
-
-    pl.semaphore_wait(barrier, expected)
-    if far:
-        @pl.when(me > 0)
-        def _():
-            pl.semaphore_wait(barrier, 1)
-
-        @pl.when(me < n_reach - 1)
-        def _():
-            pl.semaphore_wait(barrier, 1)
-    for m in range(members):
+            pack(0, m, c, lam[m, c])
+        if m == 0:
+            pl.semaphore_wait(barrier, expected)
+            if far:
+                @pl.when(me > 0)
+                def _():
+                    pl.semaphore_wait(barrier, 1)
+
+                @pl.when(me < n_reach - 1)
+                def _():
+                    pl.semaphore_wait(barrier, 1)
         send(0, m)
 
     @pl.when(me == 0)
@@ -145,6 +163,8 @@
     def _():
         rcv[:, 1] = jnp.zeros(rcv.shape[:1] + rcv.shape[2:], F32)
 
+    for copy in tables_in:
+        copy.wait()
     wet = wet_ref[...].astype(F32)
     wet_dt = TIME_STEP * wet
     patch_row = lax.broadcasted_iota(jnp.int32, (npatch, elems), 0)
@@ -178,85 +198,116 @@
     first = None
     for m in range(members):
         for c in range(1, comps):
-            term = work(m, c, adj_ref[m, c])
+            term = work(m, c, lam[m, c])
             first = term if first is None else first + term
     acc[...] = first
 
-    mix = [[[mix_ref[d, a, c] for c in range(comps)] for a in range(comps)] for d in range(2)]
-
-    def body(stage, src, m):
-        receive(stage, m)
-        state = [src[m, c] for c in range(comps)]
+    slot_lanes = 128
+    chunk = min(npatch, 128)
+    tri = jnp.where(
+        lax.broadcasted_iota(jnp.int32, (chunk, chunk), 0)
+        < lax.broadcasted_iota(jnp.int32, (chunk, chunk), 1), 1.0, 0.0,
+    )
+    slot = lax.broadcasted_iota(jnp.int32, (slot_lanes, chunk), 0).astype(F32)
+    before = jnp.zeros((1, 1), F32)
+    for k in range(npatch // chunk):
+        mine = jnp.where(po_ref[:, k * chunk:(k + 1) * chunk] == me, 1.0, 0.0)
+        rank = jnp.dot(jnp.broadcast_to(mine, (8, chunk)), tri, preferred_element_type=F32)[0:1] + before
+        table[k] = jnp.where(slot == rank, 1.0, 0.0) * mine
+        before = before + jnp.sum(mine, axis=1, keepdims=True)
+
+    mix = [[[mix_ref[a, d, c] for c in range(comps)] for a in range(comps)] for d in range(2)]
+
+    last = 2 * STEPS - 1
+
+    def stage_group(stage, group):
+        for m in group:
+            receive(stage, m)
+        half = stage % 2
+        src = lam if half == 0 else hal
+        states = [[src[m, c] for c in range(comps)] for m in group]
         ghost = []
-        for c in range(comps):
-            west = rcv[stage, 0, m, c * prows:(c + 1) * prows, :]
-            east = rcv[stage, 1, m, c * prows:(c + 1) * prows, :]
-            for g in range(groups):
-                a, b = (-RIVW * g) % elems, (elems - RIVW - RIVW * g) % elems
-                wr = pltpu.roll(west, a, 1) if a else west
-                er = pltpu.roll(east, b, 1) if b else east
-                ghost.append(jnp.where(lane < elems // 2, wr, er))
+        for m in group:
+            for c in range(comps):
+                west = rcv[stage, 0, m, c * prows:(c + 1) * prows, :]
+                east = rcv[stage, 1, m, c * prows:(c + 1) * prows, :]
+                for g in range(groups):
+                    a, b = (-RIVW * g) % elems, (elems - RIVW - RIVW * g) % elems
+                    wr = pltpu.roll(west, a, 1) if a else west
+                    er = pltpu.roll(east, b, 1) if b else east
+                    ghost.append(jnp.where(lane < elems // 2, wr, er))
+        flat = [x for state in states for x in state]
         full = jnp.concatenate(
-            [jnp.concatenate(state, axis=0), jnp.concatenate(ghost, axis=0)], axis=1
+            [jnp.concatenate(flat, axis=0), jnp.concatenate(ghost, axis=0)], axis=1
         )
         hi, lo = split_two(full)
         jump = jnp.dot(hi, sel[...], preferred_element_type=F32)
         jump = jump + jnp.dot(lo, sel[...], preferred_element_type=F32)
         cols_hi, cols_lo = [], []
-        for c in range(comps):
-            pieces = []
-            for d in range(2):
-                z = mix[d][0][c] * state[0] + mix[d][1][c] * state[1] + mix[d][2][c] * state[2]
-                pieces.append(dscale[d:d + 1, :] * z)
-            for f in range(4):
-                pieces.append(
-                    dscale[2 + f:3 + f, :]
-                    * jump[c * nodes:(c + 1) * nodes, f * elems:(f + 1) * elems]
-                )
-            data = jnp.concatenate(pieces, axis=0)
-            dh, dl = split_two(data)
-            cols_hi.append(dh)
-            cols_lo.append(dl)
+        for i, state in enumerate(states):
+            for c in range(comps):
+                pieces = []
+                for d in range(2):
+                    z = mix[d][0][c] * state[0] + mix[d][1][c] * state[1] + mix[d][2][c] * state[2]
+                    pieces.append(dscale[d:d + 1, :] * z)
+                r = (i * comps + c) * nodes
+                for f in range(4):
+                    pieces.append(
+                        dscale[2 + f:3 + f, :] * jump[r:r + nodes, f * elems:(f + 1) * elems]
+                    )
+                data = jnp.concatenate(pieces, axis=0)
+                dh, dl = split_two(data)
+                cols_hi.append(dh)
+                cols_lo.append(dl)
         data_hi = jnp.concatenate(cols_hi, axis=1)
         data_lo = jnp.concatenate(cols_lo, axis=1)
         both = jnp.dot(w_all[...], data_hi, preferred_element_type=F32)
         total = both[:nodes] + both[nodes:]
         total = total + jnp.dot(w_all[0:nodes, :], data_lo, preferred_element_type=F32)
-        moved = []
-        for c in range(comps):
-            inc = total[:, c * elems:(c + 1) * elems]
-            if c > 0:
-                inc = inc - damp[...] * state[c]
-            moved.append(state[c] + inc)
-        return moved
-
-    last = 2 * STEPS - 1
-
-    def stage_member(stage, m):
-        step, half = divmod(stage, 2)
-        base = adj_ref if step == 0 else lam
-        if half == 0:
-            new = body(stage, base, m)
+        results = []
+        for i, (m, state) in enumerate(zip(group, states)):
+            new = []
             for c in range(comps):
-                hal[m, c] = new[c]
+                k = i * comps + c
+                inc = total[:, k * elems:(k + 1) * elems]
+                if c > 0:
+                    inc = inc - damp[...] * state[c]
+                moved = state[c] + inc
+                if half:
+                    moved = 0.5 * lam[m, c] + 0.5 * moved
+                new.append(moved)
+            results.append(new)
+        dst = lam if half else hal
+        for m, new in zip(group, results):
+            for c in range(comps):
+                if stage < last:
+                    pack(stage + 1, m, c, new[c])
+                dst[m, c] = new[c]
+            if stage < last:
+                send(stage + 1, m)
+            else:
+                out_copy(m).start()
+        if stage < last:
+            terms = acc[...]
+            for m, new in zip(group, results):
+                terms = terms + (work(m, 1, new[1]) + work(m, 2, new[2]))
+            acc[...] = terms
+
+    def out_copy(m):
+        return pltpu.make_async_copy(lam.at[m], out_ref.at[m], out_sem.at[m])
+
+    def run(stage, lo, hi):
+        size = min(GROUP, hi - lo)
+
+        def step(i, carry):
+            stage_group(stage, [lo + i * size + k for k in range(size)])
+            return carry
+
+        count = (hi - lo) // size
+        if count == 1:
+            step(0, 0)
         else:
-            new = body(stage, hal, m)
-            new = [0.5 * base[m, c] + 0.5 * new[c] for c in range(comps)]
-            dst = out_ref if stage == last else lam
-            for c in range(comps):
-                dst[m, c] = new[c]
-        if stage < last:
-            for c in range(comps):
-                pack(stage + 1, m, c, new[c])
-            send(stage + 1, m)
-            acc[...] += work(m, 1, new[1]) + work(m, 2, new[2])
-
-    def run(stage, lo, hi):
-        def step(m, carry):
-            stage_member(stage, m)
-            return carry
-
-        lax.fori_loop(lo, hi, step, 0)
+            lax.fori_loop(0, count, step, 0)
 
     def patch_copy(phase, k):
         mine = phases[phase][2]
@@ -292,33 +343,23 @@
         precision=FINEST, preferred_element_type=F32,
     )
     patch_send(0, sums)
-    half_way = members // 2
+    half_way = min(1, members)
     run(last, 0, half_way)
     for phase in range(1, len(phases)):
         patch_send(phase, patch_sum(phase - 1))
     run(last, half_way, members)
     sums = patch_sum(len(phases) - 1) * (1.0 / (members_all * nodes))
 
-    slot_lanes = 128
-    chunk = min(npatch, 128)
-    tri = jnp.where(
-        lax.broadcasted_iota(jnp.int32, (chunk, chunk), 0)
-        < lax.broadcasted_iota(jnp.int32, (chunk, chunk), 1), 1.0, 0.0,
-    )
-    slot = lax.broadcasted_iota(jnp.int32, (slot_lanes, chunk), 0).astype(F32)
-    before = jnp.zeros((1, 1), F32)
     result = jnp.zeros((8, slot_lanes), F32)
     for k in range(npatch // chunk):
-        mine = jnp.where(po_ref[:, k * chunk:(k + 1) * chunk] == me, 1.0, 0.0)
-        rank = jnp.dot(jnp.broadcast_to(mine, (8, chunk)), tri, preferred_element_type=F32)[0:1] + before
-        table = jnp.where(slot == rank, 1.0, 0.0) * mine
         result = result + lax.dot_general(
-            sums[:, k * chunk:(k + 1) * chunk], table, (((1,), (1,)), ((), ())),
+            sums[:, k * chunk:(k + 1) * chunk], table[k], (((1,), (1,)), ((), ())),
             precision=FINEST, preferred_element_type=F32,
         )
-        before = before + jnp.sum(mine, axis=1, keepdims=True)
     own_ref[...] = result[0:1, :OWN_MAX]
 
+    for m in range(members):
+        out_copy(m).wait()
     for stage in range(2 * STEPS):
         for m in range(members):
             @pl.when(me < n_reach - 1)
@@ -344,8 +385,7 @@
     prow = comps * nodes * RIVW // elems
     sizes = [n_ens] + radices(n_reach)
     vmem = pl.BlockSpec(memory_space=pltpu.VMEM)
-    specs = [vmem] * 13
-    specs[8] = pl.BlockSpec(memory_space=pltpu.SMEM)
+    specs = [pl.BlockSpec(memory_space=pltpu.HBM)] * 13
     finals, owned = pl.pallas_call(
         functools.partial(kernel, n_reach, n_ens, members * n_ens),
         out_shape=(
@@ -353,8 +393,21 @@
             jax.ShapeDtypeStruct((1, OWN_MAX), F32),
         ),
         in_specs=specs,
-        out_specs=(vmem, vmem),
+        out_specs=(pl.BlockSpec(memory_space=pltpu.HBM), vmem),
         scratch_shapes=[
+            pltpu.VMEM(momentum.shape, momentum.dtype),
+            pltpu.VMEM(friction.shape, F32),
+            pltpu.VMEM((1, npatch), F32),
+            pltpu.VMEM(geometry.shape, F32),
+            pltpu.VMEM(face_scale.shape, F32),
+            pltpu.VMEM(vol_blocks.shape, F32),
+            pltpu.VMEM(face_blocks.shape, F32),
+            pltpu.SMEM((comps, 2, comps), F32),
+            pltpu.VMEM(neighbours.shape, jnp.int32),
+            pltpu.VMEM((1, elems), jnp.int32),
+            pltpu.VMEM((1, npatch), jnp.int32),
+            pltpu.VMEM((1, elems), jnp.int32),
+            pltpu.SemaphoreType.DMA((members + 12,)),
             pltpu.VMEM(adjoint.shape, F32),
             pltpu.VMEM(adjoint.shape, F32),
             pltpu.VMEM((nodes, elems), F32),
@@ -371,13 +424,15 @@
             pltpu.SemaphoreType.DMA((stages, 2, members)),
             pltpu.SemaphoreType.DMA((len(sizes), max(sizes))),
             pltpu.SemaphoreType.DMA((len(sizes), max(sizes))),
+            pltpu.VMEM((max(npatch // 128, 1), 128, min(npatch, 128)), F32),
+            pltpu.SemaphoreType.DMA((members,)),
         ],
         compiler_params=pltpu.CompilerParams(
-            collective_id=0, has_side_effects=True, vmem_limit_bytes=40 * 1024 * 1024
+            collective_id=0, has_side_effects=True, vmem_limit_bytes=60 * 1024 * 1024
         ),
     )(
         adjoint, momentum, friction, roughness.reshape(1, npatch), geometry, face_scale,
-        vol_blocks, face_blocks, flux_mix, neighbours, patch_map.reshape(1, elems),
+        vol_blocks, face_blocks, flux_mix.transpose(1, 0, 2), neighbours, patch_map.reshape(1, elems),
         patch_owner.reshape(1, npatch), wet.reshape(1, elems),
     )
     return finals, owned.reshape(OWN_MAX)

time: 39.3 us -> 34.3 us (0.87)
  local copies, waits for them, and re-layouts: 7.05 us -> 2.28 us
    unnamed x29 -> x4, local copies, waits for them, and re-layouts: 7.05 us -> 2.28 us
where the time goes in v1:
time: 34.3 us; the launch traced here: 34.2 us
  Pallas kernels  31.3 us (91%)
  local copies, waits for them, and re-layouts  2.28 us (7%)
  between operations  0.65 us (2%)
    pallas_call x1, Pallas kernels, shards(): pl.pallas_call(functools.partial(kernel, n_reach, n_ens, members * n_ens)...  31.3 us
    unnamed x4, local copies, waits for them, and re-layouts  2.28 us

profile of v1, /device:TPU:0, one launch (start us, length us, event | category | flops | bytes accessed | tf_op | source)
XLA Modules:
  0.0 34.2 jit_solution(9445434487082270673)
XLA Ops:
  0.6 31.3 %shard_map.140 = (f32[4,3,64,128]{3,2,1,0:T(8,128)}, f32[1,32]{1,0:T(1,128)}) custom-call(f32[4,3,64,128]{3,2,1,0:T(8,128)} %adj_hbm.1, bf16[4,2,64,128]{3,2,1,0:T(8,128)(2,1)} %mom_hbm.1, f32[64,128]{1,0:T(8,128)} %fric_hbm.1, f32[1,128]{1,0:T(1,128)} %bitcast.7, f32[2,128]{1,0:T(2,128)} %geo_hbm.1, f32[4,128]{1,0:T(4,128)} %face_hbm.1, ...), custom_call_target="tpu_custom_call" | custom-call | tf_op jit(solution)/shard_map/pallas_call | solution.py:389
  31.9 0.0 copy-start
  31.9 1.8 %copy.17 = f32[4,3,64,128]{3,2,1,0:T(8,128)} copy(f32[4,3,64,128]{3,2,1,0:T(8,128)} %get-tuple-element.8) | data formatting | bytes 786432
  33.7 0.0 copy-done
  33.7 0.5 %copy.18 = f32[32]{0:T(128)} copy(f32[32]{0:T(128)S(1)} %bitcast.11) | data formatting | bytes 256
Async XLA Ops:
  31.9 1.8 %copy-start = (f32[1,32]{1,0:T(1,128)S(1)}, f32[1,32]{1,0:T(1,128)}, u32[]{:S(2)}) copy-start(f32[1,32]{1,0:T(1,128)} %get-tuple-element.5) | copy-start | bytes 388

commit v2 on v1

--- a/solution.py
+++ b/solution.py
@@ -51,6 +51,9 @@
     digits = radices(n_reach)
 
     phases = [("ens", n_ens, my_ens, 1)]
+    if n_reach * n_ens <= 32:
+        phases = [("both", n_reach * n_ens, me * n_ens + my_ens, 1)]
+        digits = []
     stride = 1
     for size in digits:
         phases.append(("reach", size, lax.rem(lax.div(me, stride), size), stride))
@@ -58,6 +61,9 @@
 
     def partner(phase, k):
         axis, size, mine, step = phases[phase]
+        if axis == "both":
+            other = lax.rem(mine + k, size)
+            return {"reach": lax.div(other, n_ens), "ens": lax.rem(other, n_ens)}
         other = lax.rem(mine + k, size)
         base = my_ens if axis == "ens" else me
         return {axis: base + (other - mine) * step}
@@ -384,6 +390,8 @@
     stages = 2 * STEPS
     prow = comps * nodes * RIVW // elems
     sizes = [n_ens] + radices(n_reach)
+    if n_reach * n_ens <= 32:
+        sizes = [n_reach * n_ens]
     vmem = pl.BlockSpec(memory_space=pltpu.VMEM)
     specs = [pl.BlockSpec(memory_space=pltpu.HBM)] * 13
     finals, owned = pl.pallas_call(

time: 34.3 us -> 33.7 us (0.983)
  Pallas kernels: 31.3 us -> 30.6 us
    pallas_call x1, Pallas kernels: 31.3 us -> 30.6 us  [shards(): pl.pallas_call(functools.partial(kernel, n_reach, n_ens, members * n_ens)...]
where the time goes in v2:
time: 33.7 us; the launch traced here: 33.6 us
  Pallas kernels  30.6 us (91%)
  local copies, waits for them, and re-layouts  2.28 us (7%)
  between operations  0.65 us (2%)
    pallas_call x1, Pallas kernels, shards(): pl.pallas_call(functools.partial(kernel, n_reach, n_ens, members * n_ens)...  30.6 us
    unnamed x4, local copies, waits for them, and re-layouts  2.28 us

profile of v2, /device:TPU:0, one launch (start us, length us, event | category | flops | bytes accessed | tf_op | source)
XLA Modules:
  0.0 33.6 jit_solution(7898076725610087068)
XLA Ops:
  0.6 30.6 %shard_map.140 = (f32[4,3,64,128]{3,2,1,0:T(8,128)}, f32[1,32]{1,0:T(1,128)}) custom-call(f32[4,3,64,128]{3,2,1,0:T(8,128)} %adj_hbm.1, bf16[4,2,64,128]{3,2,1,0:T(8,128)(2,1)} %mom_hbm.1, f32[64,128]{1,0:T(8,128)} %fric_hbm.1, f32[1,128]{1,0:T(1,128)} %bitcast.7, f32[2,128]{1,0:T(2,128)} %geo_hbm.1, f32[4,128]{1,0:T(4,128)} %face_hbm.1, ...), custom_call_target="tpu_custom_call" | custom-call | tf_op jit(solution)/shard_map/pallas_call | solution.py:397
  31.3 0.0 copy-start
  31.3 1.8 %copy.17 = f32[4,3,64,128]{3,2,1,0:T(8,128)} copy(f32[4,3,64,128]{3,2,1,0:T(8,128)} %get-tuple-element.8) | data formatting | bytes 786432
  33.0 0.0 copy-done
  33.0 0.5 %copy.18 = f32[32]{0:T(128)} copy(f32[32]{0:T(128)S(1)} %bitcast.11) | data formatting | bytes 256
Async XLA Ops:
  31.3 1.8 %copy-start = (f32[1,32]{1,0:T(1,128)S(1)}, f32[1,32]{1,0:T(1,128)}, u32[]{:S(2)}) copy-start(f32[1,32]{1,0:T(1,128)} %get-tuple-element.5) | copy-start | bytes 388
